TPU v7x, 32 devices: a whole 2x2x4 slice. The times are simulated.
32 devices in a mesh: space: 8 (over y, x, core), chan: 4 (over z).
Axes of the slice: x: 2, y: 2, z: 4, core: 2. Of those that a mesh axis runs over, the one named last changes fastest.
Arguments:
- field: bfloat16 [96, 768, 32], P('chan', 'space'), may hold values from -6 to 6
- grad_out: bfloat16 [96, 768, 32], P('chan', 'space'), may hold values from -6 to 6
- filters: bfloat16 [9, 96, 96], replicated, may hold values from -0.21875 to 0.21875
Outputs:
- grad_field: float32 [96, 768, 32], P('chan', 'space')
- grad_filters: float32 [9, 96, 96], P(None, 'chan')
All inputs are finite; a program needn't handle non-finite values.
Results may differ from a plain program's by a relative error of at most 0.0003.
Values may be sent and summed in bfloat16 or wider, within the bound.
A program may use at most 64 MiB of HBM per device.

v0:
```python
import math

import jax
import jax.numpy as jnp
from jax import lax
from jax.sharding import PartitionSpec as P


def with_halo(cells, sides, width):
    for axis, dim in sides:
        count = lax.axis_size(axis)
        ends = count - 1
        head = lax.slice_in_dim(cells, 0, width, axis=dim)
        tail = lax.slice_in_dim(cells, cells.shape[dim] - width, cells.shape[dim], axis=dim)
        cells = jnp.concatenate(
            [
                lax.ppermute(tail, axis, [(i, (i + 1) % count) for i in range(ends)]),
                cells,
                lax.ppermute(head, axis, [((i + 1) % count, i) for i in range(ends)]),
            ],
            axis=dim,
        )
    return cells


def tap_terms(source, weights, padded, width, rows):
    result = jnp.zeros((weights.shape[1], width, rows), jnp.float32)
    parts = []
    for a in range(3):
        for b in range(3):
            k = a * 3 + b
            shifted = padded[:, 4 - 2 * a : 4 - 2 * a + width, 4 - 2 * b : 4 - 2 * b + rows]
            result = result + jnp.einsum(
                "io,owr->iwr", weights[k], shifted, preferred_element_type=jnp.float32
            )
            parts.append(
                jnp.einsum("iwr,owr->io", source, shifted, preferred_element_type=jnp.float32)
            )
    return (result, jnp.stack(parts))


def per_device(field, grad_out, filters):
    chan_dev = field.shape[0]
    width = field.shape[1]
    rows = field.shape[2]
    factor = 1.0 / math.sqrt(rows * width * lax.axis_size("space"))
    bordered = with_halo(grad_out, (("space", 1),), 2)
    first = lax.axis_index("chan") * chan_dev
    mine = lax.dynamic_slice_in_dim(filters, first, chan_dev, 1)
    padded = jnp.pad(lax.all_gather(bordered, "chan", axis=0, tiled=True), ((0, 0), (0, 0), (2, 2)))
    result, parts = tap_terms(field, mine, padded, width, rows)
    total = lax.psum(parts, "space")
    return (result, total * factor)


def solution(mesh):
    in_specs = (P("chan", "space", None), P("chan", "space", None), P())
    out_specs = (P("chan", "space", None), P(None, "chan", None))
    return jax.shard_map(
        per_device, mesh=mesh, in_specs=in_specs, out_specs=out_specs, check_vma=False
    )
```

profile of v0, /device:TPU:0, one launch (start us, length us, event | category | flops | bytes accessed | tf_op | source)
XLA Modules:
  0.0 103.3 jit_solution(4172286919228093528)
XLA Ops:
  7.2 0.0 copy-start
  7.2 0.0 all-reduce.3.cloned.1.call-start
  7.2 1.1 %copy.5 = bf16[24,96,32]{1,0,2:T(8,128)(2,1)S(1)} copy(bf16[24,96,32]{1,2,0:T(8,128)(2,1)} %param.4) | data formatting | bytes 294912 | tf_op args[1]
  8.3 0.1 fusion.70
  8.4 2.4 %collective-permute-start = (bf16[24,2,32]{1,0,2:T(8,128)(2,1)S(1)}, bf16[24,2,32]{1,0,2:T(8,128)(2,1)S(1)}, u32[]{:S(2)}, u32[]{:S(2)}) collective-permute-start(bf16[24,2,32]{1,0,2:T(8,128)(2,1)S(1)} %get-tuple-element.4), channel_id=1, source_target_pairs={{0,4},{4,8},{8,12},{12,16},{16,20},{20,24},{24,28},{1,5},{5,9},{9,... | collective-permute-start | bytes 9224 | tf_op jit(solution)/shard_map/ppermute | solution.py:17
  10.8 1.3 %collective-permute-start.1 = (bf16[24,2,32]{1,0,2:T(8,128)(2,1)S(1)}, bf16[24,2,32]{1,0,2:T(8,128)(2,1)S(1)}, u32[]{:S(2)}, u32[]{:S(2)}) collective-permute-start(bf16[24,2,32]{1,0,2:T(8,128)(2,1)S(1)} %get-tuple-element.5), channel_id=1, source_target_pairs={{4,0},{8,4},{12,8},{16,12},{20,16},{24,20},{28,24},{5,1},{9,5},{13... | collective-permute-start | bytes 9224 | tf_op jit(solution)/shard_map/ppermute | solution.py:19
  12.1 0.0 collective-permute-done
  12.1 4.1 %collective-permute-done.1 = bf16[24,2,32]{1,0,2:T(8,128)(2,1)S(1)} collective-permute-done((bf16[24,2,32]{1,0,2:T(8,128)(2,1)S(1)}, bf16[24,2,32]{1,0,2:T(8,128)(2,1)S(1)}, u32[]{:S(2)}, u32[]{:S(2)}) %collective-permute-start.1) | collective-permute-done | bytes 3104 | tf_op jit(solution)/shard_map/ppermute | solution.py:19
  16.2 0.2 pad_maximum_fusion
  16.4 0.0 copy-start.2
  16.4 17.8 %all_gather.3 = bf16[96,100,32]{1,0,2:T(8,128)(2,1)S(1)} all-gather(bf16[24,100,32]{1,0,2:T(8,128)(2,1)S(1)} %pad_maximum_fusion), channel_id=1, replica_groups=mesh['space'=8,'chan'=4] {'chan'}, dimensions={0}, use_global_device_ids=true | all-gather | bytes 768000 | tf_op jit(solution)/shard_map/all_gather | solution.py:50
  34.2 0.0 copy-done.2
  34.2 0.5 fusion.8
  34.7 0.4 fusion.7
  35.1 0.5 fusion.6
  35.6 0.5 fusion.5
  36.1 0.4 fusion.4
  36.5 0.5 fusion.3
  37.0 0.4 fusion.2
  37.4 0.4 fusion.1
  37.7 0.4 fusion
  38.1 0.0 copy-start.1
  38.1 0.7 copy-done.1
  38.8 0.0 all-reduce.3.cloned.1.call-update
  38.8 0.0 copy-done
  38.8 0.4 fusion.26
  39.2 0.4 convolution_add_fusion.7
  39.6 0.4 convolution_add_fusion.6
  40.0 0.4 convolution_add_fusion.5
  40.5 0.4 convolution_add_fusion.4
  40.9 0.4 convolution_add_fusion.3
  41.3 0.2 convolution_add_fusion.2
  41.5 0.2 convolution_add_fusion.1
  41.7 0.2 convolution_add_fusion
  42.0 0.8 copy.17
  42.8 52.1 %all-reduce.3.cloned.1.call-done = f32[9,24,96]{2,1,0:T(8,128)} async-done(((f32[9,24,96]{2,1,0:T(8,128)}), f32[9,24,96]{2,1,0:T(8,128)}) %all-reduce.3.cloned.1.call-update) | async-done | bytes 82960 | tf_op jit(solution)/shard_map/psum | solution.py:52
  94.9 1.6 %broadcast_multiply_fusion = f32[9,24,96]{2,1,0:T(8,128)} fusion(f32[9,24,96]{2,1,0:T(8,128)} %all-reduce.3.cloned.1.call-done), kind=kLoop, calls=%fused_computation.58 | loop fusion | flops 20736 | bytes 165888 | tf_op jit(solution)/shard_map/mul | solution.py:53
Async XLA Ops:
  7.2 31.6 %copy-start = (bf16[9,96,96]{2,1,0:T(8,128)(2,1)S(1)}, bf16[9,96,96]{2,1,0:T(8,128)(2,1)}, u32[]{:S(2)}) copy-start(bf16[9,96,96]{2,1,0:T(8,128)(2,1)} %param.5) | copy-start | bytes 497668
  7.2 87.7 %all-reduce.3.cloned.1.call-start = ((), (), s32[]{:S(2)}) async-start(), calls=%async_computation | async-start | bytes 221184 | tf_op jit(solution)/shard_map/psum | solution.py:52
  8.4 3.7 %collective-permute-start = (bf16[24,2,32]{1,0,2:T(8,128)(2,1)S(1)}, bf16[24,2,32]{1,0,2:T(8,128)(2,1)S(1)}, u32[]{:S(2)}, u32[]{:S(2)}) collective-permute-start(bf16[24,2,32]{1,0,2:T(8,128)(2,1)S(1)} %get-tuple-element.4), channel_id=1, source_target_pairs={{0,4},{4,8},{8,12},{12,16},{16,20},{20,24},{24,28},{1,5},{5,9},{9,... | collective-permute-start | bytes 9224 | tf_op jit(solution)/shard_map/ppermute | solution.py:17
  10.8 5.4 %collective-permute-start.1 = (bf16[24,2,32]{1,0,2:T(8,128)(2,1)S(1)}, bf16[24,2,32]{1,0,2:T(8,128)(2,1)S(1)}, u32[]{:S(2)}, u32[]{:S(2)}) collective-permute-start(bf16[24,2,32]{1,0,2:T(8,128)(2,1)S(1)} %get-tuple-element.5), channel_id=1, source_target_pairs={{4,0},{8,4},{12,8},{16,12},{20,16},{24,20},{28,24},{5,1},{9,5},{13... | collective-permute-start | bytes 9224 | tf_op jit(solution)/shard_map/ppermute | solution.py:19
  16.4 17.8 %copy-start.2 = (bf16[24,96,32]{1,2,0:T(8,128)(2,1)S(1)}, bf16[24,96,32]{1,2,0:T(8,128)(2,1)}, u32[]{:S(2)}) copy-start(bf16[24,96,32]{1,2,0:T(8,128)(2,1)} %param.3) | copy-start | bytes 442372
  38.1 0.7 copy-start.1
Sparse Core Ops, SparseCore 0:
  38.9 55.9 all-reduce.2
where the time goes:
time: 104 us; the launch traced here: 103 us
  waiting for transfers between devices  56.3 us (54%)
  blocking collectives  17.8 us (17%)
  between operations  14.2 us (14%)
  matrix products  6.95 us (7%)
  starting transfers between devices  3.7 us (4%)
  local copies, waits for them, and re-layouts  2.68 us (3%)
  other arithmetic  1.74 us (2%)
    psum x1, waiting for transfers between devices, per_device(): total = lax.psum(parts, 'space')  52.1 us
    all_gather x1, blocking collectives, per_device(): lax.all_gather(bordered, 'chan', axis=0, tiled=True)  17.8 us
    ppermute x1, waiting for transfers between devices, with_halo(): lax.ppermute(head, axis, [((i + 1) % count, i) for i in range(ends)])  4.12 us
    dot_general x9, matrix products, tap_terms(): jnp.einsum('iwr,owr->io', source, shifted, preferred_element_type=jnp.flo...  3.82 us
    dot_general x9, matrix products, tap_terms(): jnp.einsum('io,owr->iwr', weights[k], shifted, preferred_element_type=jnp...  3.13 us
    unnamed x8, local copies, waits for them, and re-layouts  2.56 us
    ppermute x1, starting transfers between devices, with_halo(): lax.ppermute(tail, axis, [(i, (i + 1) % count) for i in range(ends)])  2.37 us
  transfers between devices with their start and end apart: 3, of which 2 were waited for; matrix products, arithmetic and copies ran while one was open for 4% of the time, Pallas kernels for 0%

commit v1 on v0

v1 whole, which is shorter than its diff:
```python
import functools
import math

import jax
import jax.numpy as jnp
from jax import lax
from jax.experimental import pallas as pl
from jax.experimental.pallas import tpu as pltpu
from jax.sharding import PartitionSpec as P

MESH = pl.DeviceIdType.MESH
F32 = jnp.float32
BF16 = jnp.bfloat16
LANES = 128
PAD = 32


def lane_index(shape):
    return lax.broadcasted_iota(jnp.int32, shape, len(shape) - 1)


def roll(x, shift):
    return pltpu.roll(x, shift % LANES, x.ndim - 1)


def row_pad(x):
    rows, chans, lanes = x.shape
    return jnp.concatenate([x, jnp.zeros((rows, PAD - chans, lanes), x.dtype)], axis=1)


def kernel(
    ns, nc, scale,
    field_ref, grad_ref, filt_ref, gf_ref, gw_ref,
    wide, wire, halo_own, halo_in, g, fa, wm, parts, rs, total,
    z_send, z_recv, h_send, h_recv, rs_send, rs_recv, ag_send, ag_recv,
):
    s = lax.axis_index("space")
    c = lax.axis_index("chan")
    chans, rows, cols = field_ref.shape
    wire_rows = rows * cols // LANES
    half = wire_rows // 2
    nq = nc * PAD
    has_left, has_right = s > 0, s < ns - 1
    has_below, has_above = c > 0, c < nc - 1

    barrier = pltpu.get_barrier_semaphore()

    def greet(space, chan):
        pl.semaphore_signal(
            barrier, inc=1, device_id={"space": space, "chan": chan}, device_id_type=MESH
        )

    for d in range(1, ns):
        greet(lax.rem(s + d, ns), c)
    for d in range(1, nc):
        other = lax.rem(c + d, nc)

        @pl.when(has_left)
        def _():
            greet(s - 1, other)

        @pl.when(has_right)
        def _():
            greet(s + 1, other)

    @pl.when(has_below)
    def _():
        greet(s, c - 1)

    @pl.when(has_above)
    def _():
        greet(s, c + 1)

    wide[...] = jnp.zeros_like(wide)
    wide[:, :, :cols] = grad_ref[...].astype(F32)
    x = wide[...]
    lane = lane_index((chans, 8, LANES))
    tail = x[:, wire_rows:, :]
    packed = jnp.concatenate(
        [
            jnp.where(lane < cols, x[:, 8 * t : 8 * t + 8, :], roll(tail, cols - 32 * t))
            for t in range(wire_rows // 8)
        ],
        axis=1,
    )
    packed = jnp.swapaxes(packed, 0, 1)
    for h in range(2):
        wire[c, h] = packed[h * half : (h + 1) * half].reshape(half * chans, LANES).astype(BF16)

    lane = lane_index(x.shape)
    y = jnp.where(lane < 2, x, 0.0) + roll(
        jnp.where((lane >= cols - 2) & (lane < cols), x, 0.0), 30 - (cols - 2)
    )
    y = jnp.swapaxes(y, 0, 1)
    count = rows
    while count > 1:
        count //= 2
        y = y[:count] + roll(y[count:], 4 * count)
    halo_own[...] = row_pad(y)[0].astype(BF16)

    greeted = (ns - 1) + (nc - 1) * (
        has_left.astype(jnp.int32) + has_right.astype(jnp.int32)
    ) + has_below.astype(jnp.int32) + has_above.astype(jnp.int32)
    pl.semaphore_wait(barrier, greeted)

    def z_copy(up, t, h):
        block = c - t if up else c + t
        way = 0 if up else 1
        return pltpu.make_async_remote_copy(
            src_ref=wire.at[block, h],
            dst_ref=wire.at[block, h],
            send_sem=z_send.at[way, t, h],
            recv_sem=z_recv.at[way, t, h],
            device_id={"space": s, "chan": c + 1 if up else c - 1},
            device_id_type=MESH,
        )

    def z_arrival(up, t, h):
        block = c - 1 - t if up else c + 1 + t
        way = 0 if up else 1
        return pltpu.make_async_remote_copy(
            src_ref=wire.at[block, h],
            dst_ref=wire.at[block, h],
            send_sem=z_send.at[way, t, h],
            recv_sem=z_recv.at[way, t, h],
            device_id={"space": s, "chan": c - 1 if up else c + 1},
            device_id_type=MESH,
        )

    def sends(up, t):
        if up:
            return has_above & (c - t >= 0)
        return has_below & (c + t < nc)

    def arrives(up, t):
        if up:
            return c - 1 - t >= 0
        return c + 1 + t < nc

    def halo_copy(right, chan):
        side = 0 if right else 1
        return pltpu.make_async_remote_copy(
            src_ref=halo_own,
            dst_ref=halo_in.at[side, c],
            send_sem=h_send.at[side, chan],
            recv_sem=h_recv.at[side, c],
            device_id={"space": s + 1 if right else s - 1, "chan": chan},
            device_id_type=MESH,
        )

    def halo_arrival(side, block):
        return pltpu.make_async_remote_copy(
            src_ref=halo_own,
            dst_ref=halo_in.at[side, block],
            send_sem=h_send.at[side, block],
            recv_sem=h_recv.at[side, block],
            device_id={"space": s - 1 if side == 0 else s + 1, "chan": block},
            device_id_type=MESH,
        )

    for h in range(2):
        for up in (True, False):

            @pl.when(sends(up, 0))
            def _():
                z_copy(up, 0, h).start()

    for right, there in ((True, has_right), (False, has_left)):

        @pl.when(there)
        def _():
            for chan in range(nc):
                halo_copy(right, chan).start()

    for side, there in ((0, has_left), (1, has_right)):

        @pl.when(jnp.logical_not(there))
        def _():
            halo_in[side] = jnp.zeros_like(halo_in[side])

    wide[:, :, :cols] = field_ref[...].astype(F32)
    f = jnp.swapaxes(wide[...], 0, 1)
    fa[...] = jnp.zeros_like(fa)
    for a in range(3):
        fa[a, 2 : 2 + rows] = row_pad(roll(f, -2 * (a - 1))).astype(BF16)

    ch = filt_ref.shape[1]
    mine = lax.broadcasted_iota(jnp.int32, (chans, ch), 0) + c * chans
    pick = (mine == lane_index((chans, ch))).astype(F32).astype(BF16)
    q = lane_index((ch, nq))
    from_q = (q // PAD) * chans + lax.rem(q, PAD)
    spread = (
        (from_q == lax.broadcasted_iota(jnp.int32, (ch, nq), 0)) & (lax.rem(q, PAD) < chans)
    ).astype(F32).astype(BF16)
    taps = [
        jnp.dot(pick, filt_ref[k], preferred_element_type=F32) for k in range(9)
    ]
    taps = jnp.concatenate(taps, axis=0).astype(BF16)
    taps = jnp.dot(taps, spread, preferred_element_type=F32)
    wm[...] = jnp.concatenate(
        [
            jnp.concatenate(
                [taps[(3 * a + b) * chans : (3 * a + b + 1) * chans] for a in range(3)], axis=0
            )
            for b in range(3)
        ],
        axis=1,
    ).astype(BF16)

    for block in range(nc):
        g[block, 0:2] = jnp.zeros((2, PAD, LANES), BF16)
        g[block, rows + 2 :] = jnp.zeros((2, PAD, LANES), BF16)

    def unpack(block):
        for side, there in ((0, has_left), (1, has_right)):

            @pl.when(there)
            def _():
                halo_arrival(side, block).wait_recv()

        w = jnp.concatenate(
            [wire[block, h].astype(F32).reshape(half, chans, LANES) for h in range(2)], axis=0
        )
        lane = lane_index((chans, LANES))
        left = halo_in[0, block].astype(F32)[:chans]
        right = halo_in[1, block].astype(F32)[:chans]
        border = jnp.where(lane % 4 < 2, right, left)
        edge = ((lane >= cols) & (lane < cols + 2)) | (lane >= LANES - 2)
        out = []
        for r in range(rows):
            if r < wire_rows:
                main = w[r]
            else:
                j = r - wire_rows
                main = jnp.zeros((chans, LANES), F32)
                for t in range(cols // 32):
                    main = jnp.where(lane // 32 == t, roll(w[8 * t + j], 32 * t - cols), main)
            rim = jnp.where(edge, roll(border, cols - 4 * r), 0.0)
            out.append(jnp.where(lane < cols, main, rim))
        g[block, 2 : 2 + rows] = row_pad(jnp.stack(out)).astype(BF16)

    unpack(c)
    for t in range(nc - 1):
        for up in (True, False):
            for h in range(2):

                @pl.when(arrives(up, t))
                def _():
                    z_arrival(up, t, h).wait_recv()

                if t + 1 < nc - 1:

                    @pl.when(sends(up, t + 1))
                    def _():
                        z_copy(up, t + 1, h).start()

        for up in (True, False):

            @pl.when(arrives(up, t))
            def _():
                unpack(c - 1 - t if up else c + 1 + t)

    def g_row(r):
        return jnp.concatenate([g[block, r] for block in range(nc)], axis=0)

    def f_row(r):
        return jnp.concatenate(
            [fa[a, r + 2 * b] for a in range(3) for b in range(3)], axis=0
        )

    acc = jnp.zeros((9 * PAD, nq), F32)
    for r in range(0, rows, 2):
        acc = acc + lax.dot_general(
            jnp.concatenate([f_row(r), f_row(r + 1)], axis=1),
            jnp.concatenate([g_row(r + 2), g_row(r + 3)], axis=1),
            (((1,), (1,)), ((), ())),
            preferred_element_type=F32,
        )
    acc = acc.reshape(9, PAD, nq)[:, :chans]
    tiles = jnp.concatenate(
        [
            acc[:, :, l * LANES : (l + 1) * LANES].reshape(9 * chans // 8, 8, LANES)
            for l in range(nq // LANES)
        ],
        axis=0,
    )
    n_tiles = tiles.shape[0]
    each = parts.shape[1]
    spare = ns * each - n_tiles
    if spare:
        tiles = jnp.concatenate([tiles, jnp.zeros((spare, 8, LANES), F32)], axis=0)
    parts[...] = tiles.reshape(ns, each, 8, LANES)

    def rs_copy(d):
        t = lax.rem(s + d, ns)
        return pltpu.make_async_remote_copy(
            src_ref=parts.at[t],
            dst_ref=rs.at[d - 1],
            send_sem=rs_send.at[d - 1],
            recv_sem=rs_recv.at[d - 1],
            device_id={"space": t, "chan": c},
            device_id_type=MESH,
        )

    def ag_copy(d):
        t = lax.rem(s + d, ns)
        return pltpu.make_async_remote_copy(
            src_ref=total.at[s],
            dst_ref=total.at[s],
            send_sem=ag_send.at[d - 1],
            recv_sem=ag_recv.at[d - 1],
            device_id={"space": t, "chan": c},
            device_id_type=MESH,
        )

    def ag_arrival(d):
        t = lax.rem(s + ns - d, ns)
        return pltpu.make_async_remote_copy(
            src_ref=total.at[t],
            dst_ref=total.at[t],
            send_sem=ag_send.at[d - 1],
            recv_sem=ag_recv.at[d - 1],
            device_id={"space": t, "chan": c},
            device_id_type=MESH,
        )

    for d in range(1, ns):
        rs_copy(d).start()

    def field_rows(first):
        out = []
        for r in range(first, first + 8, 2):
            operand = jnp.concatenate(
                [
                    jnp.concatenate([g_row(r + 4 - 2 * b), g_row(r + 5 - 2 * b)], axis=1)
                    for b in range(3)
                ],
                axis=0,
            )
            p = jnp.dot(wm[...], operand, preferred_element_type=F32)
            for j in range(2):
                part = p[:, j * LANES : (j + 1) * LANES]
                out.append(
                    sum(
                        roll(part[a * chans : (a + 1) * chans], 2 * (a - 1)) if a != 1
                        else part[a * chans : (a + 1) * chans]
                        for a in range(3)
                    )
                )
        out = jnp.swapaxes(jnp.stack(out), 0, 1)
        gf_ref[:, first : first + 8, :] = out[:, :, :cols]

    middle = rows // 2
    for first in range(0, middle, 8):
        field_rows(first)

    mine_total = parts[s]
    for d in range(1, ns):
        rs_copy(d).wait_recv()
        mine_total = mine_total + rs[d - 1]
    total[s] = mine_total * scale
    for d in range(1, ns):
        ag_copy(d).start()

    for first in range(middle, rows, 8):
        field_rows(first)

    for d in range(1, ns):
        ag_arrival(d).wait_recv()
    tiles = total[...].reshape(ns * each, 8, LANES)
    group = 9 * chans // 8
    per_lane = [
        tiles[l * group : (l + 1) * group].reshape(9, chans, LANES) for l in range(nq // LANES)
    ]
    spaced = per_lane[0] if len(per_lane) == 1 else jnp.concatenate(per_lane, axis=2)
    gw_ref[...] = jnp.concatenate(
        [spaced[:, :, b * PAD : b * PAD + chans] for b in range(nc)], axis=2
    )

    for t in range(nc - 1):
        for up in (True, False):

            @pl.when(sends(up, t))
            def _():
                for h in range(2):
                    z_copy(up, t, h).wait_send()

    for right, there in ((True, has_right), (False, has_left)):

        @pl.when(there)
        def _():
            for chan in range(nc):
                halo_copy(right, chan).wait_send()

    for d in range(1, ns):
        rs_copy(d).wait_send()
        ag_copy(d).wait_send()


def per_device(ns, nc, field, grad_out, filters):
    chans, cols, rows = field.shape
    wire_rows = rows * cols // LANES
    nq = nc * PAD
    ch = filters.shape[1]
    n_tiles = (9 * chans // 8) * (nq // LANES)
    each = -(-n_tiles // ns)
    scale = 1.0 / math.sqrt(rows * cols * ns)
    vmem = pl.BlockSpec(memory_space=pltpu.VMEM)
    dma = pltpu.SemaphoreType.DMA
    gf, gw = pl.pallas_call(
        functools.partial(kernel, ns, nc, scale),
        out_shape=(
            jax.ShapeDtypeStruct((chans, rows, cols), F32),
            jax.ShapeDtypeStruct((9, chans, ch), F32),
        ),
        in_specs=[vmem] * 3,
        out_specs=(vmem, vmem),
        scratch_shapes=[
            pltpu.VMEM((chans, rows, LANES), F32),
            pltpu.VMEM((nc, 2, wire_rows // 2 * chans, LANES), BF16),
            pltpu.VMEM((PAD, LANES), BF16),
            pltpu.VMEM((2, nc, PAD, LANES), BF16),
            pltpu.VMEM((nc, rows + 4, PAD, LANES), BF16),
            pltpu.VMEM((3, rows + 4, PAD, LANES), BF16),
            pltpu.VMEM((3 * chans, 3 * nq), BF16),
            pltpu.VMEM((ns, each, 8, LANES), F32),
            pltpu.VMEM((ns - 1, each, 8, LANES), F32),
            pltpu.VMEM((ns, each, 8, LANES), F32),
            dma((2, nc - 1, 2)),
            dma((2, nc - 1, 2)),
            dma((2, nc)),
            dma((2, nc)),
            dma((ns - 1,)),
            dma((ns - 1,)),
            dma((ns - 1,)),
            dma((ns - 1,)),
        ],
        compiler_params=pltpu.CompilerParams(
            collective_id=0, has_side_effects=True, vmem_limit_bytes=40 * 1024 * 1024
        ),
        cost_estimate=pl.CostEstimate(
            flops=4 * 9 * chans * ch * rows * cols, bytes_accessed=2 * 1024 * 1024, transcendentals=0
        ),
    )(jnp.swapaxes(field, 1, 2), jnp.swapaxes(grad_out, 1, 2), filters)
    return jnp.swapaxes(gf, 1, 2), gw


def solution(mesh):
    ns, nc = mesh.shape["space"], mesh.shape["chan"]
    in_specs = (P("chan", "space", None), P("chan", "space", None), P())
    out_specs = (P("chan", "space", None), P(None, "chan", None))
    return jax.shard_map(
        functools.partial(per_device, ns, nc),
        mesh=mesh, in_specs=in_specs, out_specs=out_specs, check_vma=False,
    )
```

time: 104 us -> 34 us (0.33)
  waiting for transfers between devices: 56.3 us -> 0 us
  Pallas kernels: 0 us -> 29 us
  blocking collectives: 17.8 us -> 0 us
  between operations: 14.2 us -> 0.65 us
  matrix products: 6.95 us -> 0 us
  starting transfers between devices: 3.7 us -> 0 us
  other arithmetic: 1.74 us -> 0 us
  local copies, waits for them, and re-layouts: 2.68 us -> 4.17 us
    psum x1 -> x0, waiting for transfers between devices: 52.1 us -> none  [per_device(): total = lax.psum(parts, 'space')]
    pallas_call x0 -> x1, Pallas kernels: none -> 29 us  [per_device(): pl.pallas_call(functools.partial(kernel, ns, nc, scale), out_shape=(jax.S...]
    all_gather x1 -> x0, blocking collectives: 17.8 us -> none  [per_device(): lax.all_gather(bordered, 'chan', axis=0, tiled=True)]
    dot_general x18 -> x0, matrix products: 6.95 us -> none  [the longest x9 3.82 us: tap_terms(): jnp.einsum('iwr,owr->io', source, shifted, preferred_element_type=jnp.flo...]
    ppermute x2 -> x0, waiting for transfers between devices: 4.12 us -> none  [the longest x1 4.12 us: with_halo(): lax.ppermute(head, axis, [((i + 1) % count, i) for i in range(ends)])]
    ppermute x2 -> x0, starting transfers between devices: 3.66 us -> none  [the longest x1 2.37 us: with_halo(): lax.ppermute(tail, axis, [(i, (i + 1) % count) for i in range(ends)])]
    unnamed x8, local copies, waits for them, and re-layouts: 2.56 us -> 4.17 us
    mul x1 -> x0, other arithmetic: 1.55 us -> none  [per_device(): return (result, total * factor)]
  transfers between devices with their start and end apart: 3 -> 0, of which waited for: 2 -> 0; matrix products, arithmetic and copies ran while one was open for 4% -> 0% of each run, Pallas kernels for 0% -> 0%
where the time goes in v1:
time: 34 us; the launch traced here: 33.8 us
  Pallas kernels  29 us (85%)
  local copies, waits for them, and re-layouts  4.17 us (12%)
  between operations  0.65 us (2%)
    pallas_call x1, Pallas kernels, per_device(): pl.pallas_call(functools.partial(kernel, ns, nc, scale), out_shape=(jax.S...  29 us
    unnamed x8, local copies, waits for them, and re-layouts  4.17 us

profile of v1, /device:TPU:0, one launch (start us, length us, event | category | flops | bytes accessed | tf_op | source)
XLA Modules:
  0.0 33.8 jit_solution(5079547962088282811)
XLA Ops:
  0.6 0.0 copy-start
  0.6 0.9 %copy-done = bf16[9,96,96]{2,1,0:T(8,128)(2,1)S(1)} copy-done((bf16[9,96,96]{2,1,0:T(8,128)(2,1)S(1)}, bf16[9,96,96]{2,1,0:T(8,128)(2,1)}, u32[]{:S(2)}) %copy-start) | copy-done | bytes 165912
  1.6 0.0 copy-start.1
  1.6 0.9 %copy-done.1 = bf16[24,96,32]{1,2,0:T(8,128)(2,1)S(1)} copy-done((bf16[24,96,32]{1,2,0:T(8,128)(2,1)S(1)}, bf16[24,96,32]{1,2,0:T(8,128)(2,1)}, u32[]{:S(2)}) %copy-start.1) | copy-done | bytes 147480
  2.5 0.0 copy-start.2
  2.5 0.9 %copy-done.2 = bf16[24,96,32]{1,2,0:T(8,128)(2,1)S(1)} copy-done((bf16[24,96,32]{1,2,0:T(8,128)(2,1)S(1)}, bf16[24,96,32]{1,2,0:T(8,128)(2,1)}, u32[]{:S(2)}) %copy-start.2) | copy-done | bytes 147480
  3.4 29.0 %shard_map.50 = (f32[24,32,96]{2,1,0:T(8,128)S(1)}, f32[9,24,96]{2,1,0:T(8,128)S(1)}) custom-call(bf16[24,32,96]{2,1,0:T(8,128)(2,1)S(1)} %bitcast.4, bf16[24,32,96]{2,1,0:T(8,128)(2,1)S(1)} %bitcast.5, bf16[9,96,96]{2,1,0:T(8,128)(2,1)S(1)} %copy-done), custom_call_target="tpu_custom_call" | custom-call | flops 254803968 | bytes 2097152 | tf_op jit(solution)/shard_map/pallas_call | solution.py:410
  32.4 0.7 %copy.7 = f32[24,96,32]{1,2,0:T(8,128)} copy(f32[24,96,32]{1,2,0:T(8,128)S(1)} %bitcast.3) | data formatting | bytes 589824
  33.2 0.6 %copy.8 = f32[9,24,96]{2,1,0:T(8,128)} copy(f32[9,24,96]{2,1,0:T(8,128)S(1)} %get-tuple-element.9) | data formatting | bytes 165888
Async XLA Ops:
  0.6 0.9 %copy-start = (bf16[9,96,96]{2,1,0:T(8,128)(2,1)S(1)}, bf16[9,96,96]{2,1,0:T(8,128)(2,1)}, u32[]{:S(2)}) copy-start(bf16[9,96,96]{2,1,0:T(8,128)(2,1)} %filt_ref.1) | copy-start | bytes 497668
  1.6 0.9 %copy-start.1 = (bf16[24,96,32]{1,2,0:T(8,128)(2,1)S(1)}, bf16[24,96,32]{1,2,0:T(8,128)(2,1)}, u32[]{:S(2)}) copy-start(bf16[24,96,32]{1,2,0:T(8,128)(2,1)} %param.3) | copy-start | bytes 442372
  2.5 0.9 %copy-start.2 = (bf16[24,96,32]{1,2,0:T(8,128)(2,1)S(1)}, bf16[24,96,32]{1,2,0:T(8,128)(2,1)}, u32[]{:S(2)}) copy-start(bf16[24,96,32]{1,2,0:T(8,128)(2,1)} %param.4) | copy-start | bytes 442372

commit v2 on v1

--- a/solution.py
+++ b/solution.py
@@ -30,13 +30,22 @@
 
 def kernel(
     ns, nc, scale,
-    field_ref, grad_ref, filt_ref, gf_ref, gw_ref,
-    wide, wire, halo_own, halo_in, g, fa, wm, parts, rs, total,
-    z_send, z_recv, h_send, h_recv, rs_send, rs_recv, ag_send, ag_recv,
+    field_hbm, grad_hbm, filt_hbm, gf_ref, gw_ref,
+    field_ref, grad_ref, filt_ref,
+    wide, wire, halo_own, halo_in, g, fa, wm, field_acc, parts, rs, total,
+    in_sem, z_send, z_recv, h_send, h_recv, rs_send, rs_recv, ag_send, ag_recv,
 ):
     s = lax.axis_index("space")
     c = lax.axis_index("chan")
     chans, rows, cols = field_ref.shape
+    loads = [
+        pltpu.make_async_copy(src, dst, in_sem.at[i])
+        for i, (src, dst) in enumerate(
+            ((grad_hbm, grad_ref), (field_hbm, field_ref), (filt_hbm, filt_ref))
+        )
+    ]
+    for load in loads:
+        load.start()
     wire_rows = rows * cols // LANES
     half = wire_rows // 2
     nq = nc * PAD
@@ -72,6 +81,7 @@
         greet(s, c + 1)
 
     wide[...] = jnp.zeros_like(wide)
+    loads[0].wait()
     wide[:, :, :cols] = grad_ref[...].astype(F32)
     x = wide[...]
     lane = lane_index((chans, 8, LANES))
@@ -178,12 +188,13 @@
         def _():
             halo_in[side] = jnp.zeros_like(halo_in[side])
 
+    loads[1].wait()
     wide[:, :, :cols] = field_ref[...].astype(F32)
     f = jnp.swapaxes(wide[...], 0, 1)
-    fa[...] = jnp.zeros_like(fa)
     for a in range(3):
-        fa[a, 2 : 2 + rows] = row_pad(roll(f, -2 * (a - 1))).astype(BF16)
-
+        fa[a] = row_pad(roll(f, -2 * (a - 1))).astype(BF16)
+
+    loads[2].wait()
     ch = filt_ref.shape[1]
     mine = lax.broadcasted_iota(jnp.int32, (chans, ch), 0) + c * chans
     pick = (mine == lane_index((chans, ch))).astype(F32).astype(BF16)
@@ -197,15 +208,17 @@
     ]
     taps = jnp.concatenate(taps, axis=0).astype(BF16)
     taps = jnp.dot(taps, spread, preferred_element_type=F32)
-    wm[...] = jnp.concatenate(
-        [
-            jnp.concatenate(
-                [taps[(3 * a + b) * chans : (3 * a + b + 1) * chans] for a in range(3)], axis=0
-            )
-            for b in range(3)
-        ],
-        axis=1,
-    ).astype(BF16)
+    for block in range(nc):
+        own = taps[:, block * PAD : (block + 1) * PAD]
+        wm[block] = jnp.concatenate(
+            [
+                jnp.concatenate(
+                    [own[(3 * a + b) * chans : (3 * a + b + 1) * chans] for b in range(3)], axis=1
+                )
+                for a in range(3)
+            ],
+            axis=0,
+        ).astype(BF16)
 
     for block in range(nc):
         g[block, 0:2] = jnp.zeros((2, PAD, LANES), BF16)
@@ -239,62 +252,45 @@
             out.append(jnp.where(lane < cols, main, rim))
         g[block, 2 : 2 + rows] = row_pad(jnp.stack(out)).astype(BF16)
 
-    unpack(c)
-    for t in range(nc - 1):
-        for up in (True, False):
-            for h in range(2):
-
-                @pl.when(arrives(up, t))
-                def _():
-                    z_arrival(up, t, h).wait_recv()
-
-                if t + 1 < nc - 1:
-
-                    @pl.when(sends(up, t + 1))
-                    def _():
-                        z_copy(up, t + 1, h).start()
-
-        for up in (True, False):
-
-            @pl.when(arrives(up, t))
-            def _():
-                unpack(c - 1 - t if up else c + 1 + t)
-
-    def g_row(r):
-        return jnp.concatenate([g[block, r] for block in range(nc)], axis=0)
-
-    def f_row(r):
+    def g_pair(block, r):
         return jnp.concatenate(
-            [fa[a, r + 2 * b] for a in range(3) for b in range(3)], axis=0
-        )
-
-    acc = jnp.zeros((9 * PAD, nq), F32)
-    for r in range(0, rows, 2):
-        acc = acc + lax.dot_general(
-            jnp.concatenate([f_row(r), f_row(r + 1)], axis=1),
-            jnp.concatenate([g_row(r + 2), g_row(r + 3)], axis=1),
-            (((1,), (1,)), ((), ())),
-            preferred_element_type=F32,
-        )
-    acc = acc.reshape(9, PAD, nq)[:, :chans]
-    tiles = jnp.concatenate(
-        [
-            acc[:, :, l * LANES : (l + 1) * LANES].reshape(9 * chans // 8, 8, LANES)
-            for l in range(nq // LANES)
-        ],
-        axis=0,
-    )
-    n_tiles = tiles.shape[0]
-    each = parts.shape[1]
-    spare = ns * each - n_tiles
+            [
+                jnp.concatenate([g[block, r + 4 - 2 * b], g[block, r + 5 - 2 * b]], axis=1)
+                for b in range(3)
+            ],
+            axis=0,
+        )
+
+    n_tiles = 3 * chans // 8
+    each = rs.shape[1]
+
+    def weight_gradient(block):
+        acc = jnp.zeros((3 * PAD, 3 * PAD), F32)
+        for r in range(0, rows, 2):
+            f_pair = jnp.concatenate(
+                [jnp.concatenate([fa[a, r], fa[a, r + 1]], axis=1) for a in range(3)], axis=0
+            )
+            acc = acc + lax.dot_general(
+                f_pair, g_pair(block, r), (((1,), (1,)), ((), ())), preferred_element_type=F32
+            )
+        acc = acc.reshape(3, PAD, 3 * PAD)[:, :chans].reshape(n_tiles, 8, 3 * PAD)
+        acc = jnp.concatenate([acc, jnp.zeros((n_tiles, 8, LANES - 3 * PAD), F32)], axis=2)
+        parts[pl.ds(block * n_tiles, n_tiles)] = acc
+
+    def field_gradient(block, first=False):
+        w = wm[block]
+        for r in range(0, rows, 2):
+            p = jnp.dot(w, g_pair(block, r), preferred_element_type=F32)
+            field_acc[r // 2] = p if first else field_acc[r // 2] + p
+
+    spare = ns * each - nc * n_tiles
     if spare:
-        tiles = jnp.concatenate([tiles, jnp.zeros((spare, 8, LANES), F32)], axis=0)
-    parts[...] = tiles.reshape(ns, each, 8, LANES)
+        parts[nc * n_tiles :] = jnp.zeros((spare, 8, LANES), F32)
 
     def rs_copy(d):
         t = lax.rem(s + d, ns)
         return pltpu.make_async_remote_copy(
-            src_ref=parts.at[t],
+            src_ref=parts.at[pl.ds(t * each, each)],
             dst_ref=rs.at[d - 1],
             send_sem=rs_send.at[d - 1],
             recv_sem=rs_recv.at[d - 1],
@@ -324,20 +320,45 @@
             device_id_type=MESH,
         )
 
-    for d in range(1, ns):
-        rs_copy(d).start()
+    unpack(c)
+    weight_gradient(c)
+    field_gradient(c, first=True)
+    for t in range(nc - 1):
+        for h in range(2):
+            for up in (True, False):
+
+                @pl.when(arrives(up, t))
+                def _():
+                    z_arrival(up, t, h).wait_recv()
+
+                if t + 1 < nc - 1:
+
+                    @pl.when(sends(up, t + 1))
+                    def _():
+                        z_copy(up, t + 1, h).start()
+
+        for up in (True, False):
+
+            @pl.when(arrives(up, t))
+            def _():
+                block = c - 1 - t if up else c + 1 + t
+                unpack(block)
+                weight_gradient(block)
+
+        if t + 1 == nc - 1:
+            for d in range(1, ns):
+                rs_copy(d).start()
+
+        for up in (True, False):
+
+            @pl.when(arrives(up, t))
+            def _():
+                field_gradient(c - 1 - t if up else c + 1 + t)
 
     def field_rows(first):
         out = []
         for r in range(first, first + 8, 2):
-            operand = jnp.concatenate(
-                [
-                    jnp.concatenate([g_row(r + 4 - 2 * b), g_row(r + 5 - 2 * b)], axis=1)
-                    for b in range(3)
-                ],
-                axis=0,
-            )
-            p = jnp.dot(wm[...], operand, preferred_element_type=F32)
+            p = field_acc[r // 2]
             for j in range(2):
                 part = p[:, j * LANES : (j + 1) * LANES]
                 out.append(
@@ -354,7 +375,7 @@
     for first in range(0, middle, 8):
         field_rows(first)
 
-    mine_total = parts[s]
+    mine_total = parts[pl.ds(s * each, each)]
     for d in range(1, ns):
         rs_copy(d).wait_recv()
         mine_total = mine_total + rs[d - 1]
@@ -368,14 +389,14 @@
     for d in range(1, ns):
         ag_arrival(d).wait_recv()
     tiles = total[...].reshape(ns * each, 8, LANES)
-    group = 9 * chans // 8
-    per_lane = [
-        tiles[l * group : (l + 1) * group].reshape(9, chans, LANES) for l in range(nq // LANES)
+    blocks = [
+        tiles[b * n_tiles : (b + 1) * n_tiles].reshape(3, chans, LANES) for b in range(nc)
     ]
-    spaced = per_lane[0] if len(per_lane) == 1 else jnp.concatenate(per_lane, axis=2)
-    gw_ref[...] = jnp.concatenate(
-        [spaced[:, :, b * PAD : b * PAD + chans] for b in range(nc)], axis=2
-    )
+    for a in range(3):
+        for b in range(3):
+            gw_ref[3 * a + b] = jnp.concatenate(
+                [block[a, :, b * PAD : b * PAD + chans] for block in blocks], axis=1
+            )
 
     for t in range(nc - 1):
         for up in (True, False):
@@ -400,9 +421,8 @@
 def per_device(ns, nc, field, grad_out, filters):
     chans, cols, rows = field.shape
     wire_rows = rows * cols // LANES
-    nq = nc * PAD
     ch = filters.shape[1]
-    n_tiles = (9 * chans // 8) * (nq // LANES)
+    n_tiles = nc * 3 * chans // 8
     each = -(-n_tiles // ns)
     scale = 1.0 / math.sqrt(rows * cols * ns)
     vmem = pl.BlockSpec(memory_space=pltpu.VMEM)
@@ -413,19 +433,24 @@
             jax.ShapeDtypeStruct((chans, rows, cols), F32),
             jax.ShapeDtypeStruct((9, chans, ch), F32),
         ),
-        in_specs=[vmem] * 3,
+        in_specs=[pl.BlockSpec(memory_space=pltpu.HBM)] * 3,
         out_specs=(vmem, vmem),
         scratch_shapes=[
+            pltpu.VMEM((chans, rows, cols), BF16),
+            pltpu.VMEM((chans, rows, cols), BF16),
+            pltpu.VMEM(filters.shape, BF16),
             pltpu.VMEM((chans, rows, LANES), F32),
             pltpu.VMEM((nc, 2, wire_rows // 2 * chans, LANES), BF16),
             pltpu.VMEM((PAD, LANES), BF16),
             pltpu.VMEM((2, nc, PAD, LANES), BF16),
             pltpu.VMEM((nc, rows + 4, PAD, LANES), BF16),
-            pltpu.VMEM((3, rows + 4, PAD, LANES), BF16),
-            pltpu.VMEM((3 * chans, 3 * nq), BF16),
-            pltpu.VMEM((ns, each, 8, LANES), F32),
+            pltpu.VMEM((3, rows, PAD, LANES), BF16),
+            pltpu.VMEM((nc, 3 * chans, 3 * PAD), BF16),
+            pltpu.VMEM((rows // 2, 3 * chans, 2 * LANES), F32),
+            pltpu.VMEM((ns * each, 8, LANES), F32),
             pltpu.VMEM((ns - 1, each, 8, LANES), F32),
             pltpu.VMEM((ns, each, 8, LANES), F32),
+            dma((3,)),
             dma((2, nc - 1, 2)),
             dma((2, nc - 1, 2)),
             dma((2, nc)),
@@ -436,7 +461,7 @@
             dma((ns - 1,)),
         ],
         compiler_params=pltpu.CompilerParams(
-            collective_id=0, has_side_effects=True, vmem_limit_bytes=40 * 1024 * 1024
+            collective_id=0, has_side_effects=True, vmem_limit_bytes=64 * 1024 * 1024
         ),
         cost_estimate=pl.CostEstimate(
             flops=4 * 9 * chans * ch * rows * cols, bytes_accessed=2 * 1024 * 1024, transcendentals=0

time: 34 us -> 31.6 us (0.929)
  local copies, waits for them, and re-layouts: 4.17 us -> 2.45 us
  Pallas kernels: 29 us -> 28.3 us
    unnamed x8 -> x4, local copies, waits for them, and re-layouts: 4.17 us -> 2.45 us
    pallas_call x1, Pallas kernels: 29 us -> 28.3 us  [per_device(): pl.pallas_call(functools.partial(kernel, ns, nc, scale), out_shape=(jax.S...]
where the time goes in v2:
time: 31.6 us; the launch traced here: 31.4 us
  Pallas kernels  28.3 us (90%)
  local copies, waits for them, and re-layouts  2.45 us (8%)
  between operations  0.65 us (2%)
    pallas_call x1, Pallas kernels, per_device(): pl.pallas_call(functools.partial(kernel, ns, nc, scale), out_shape=(jax.S...  28.3 us
    unnamed x4, local copies, waits for them, and re-layouts  2.45 us

profile of v2, /device:TPU:0, one launch (start us, length us, event | category | flops | bytes accessed | tf_op | source)
XLA Modules:
  0.0 31.4 jit_solution(7160381190691405871)
XLA Ops:
  0.6 28.3 %shard_map.50 = (f32[24,32,96]{2,1,0:T(8,128)}, f32[9,24,96]{2,1,0:T(8,128)}) custom-call(bf16[24,32,96]{2,1,0:T(8,128)(2,1)} %bitcast.4, bf16[24,32,96]{2,1,0:T(8,128)(2,1)} %bitcast.5, bf16[9,96,96]{2,1,0:T(8,128)(2,1)} %filt_hbm.1), custom_call_target="tpu_custom_call" | custom-call | flops 254803968 | bytes 2097152 | tf_op jit(solution)/shard_map/pallas_call | solution.py:430
  29.0 0.0 copy-start
  29.0 1.8 %copy.7 = f32[24,96,32]{1,2,0:T(8,128)} copy(f32[24,96,32]{1,2,0:T(8,128)} %bitcast.3) | data formatting | bytes 589824
  30.8 0.0 copy-done
  30.8 0.6 %copy.8 = f32[9,24,96]{2,1,0:T(8,128)} copy(f32[9,24,96]{2,1,0:T(8,128)S(1)} %copy-done) | data formatting | bytes 165888
Async XLA Ops:
  29.0 1.8 %copy-start = (f32[9,24,96]{2,1,0:T(8,128)S(1)}, f32[9,24,96]{2,1,0:T(8,128)}, u32[]{:S(2)}) copy-start(f32[9,24,96]{2,1,0:T(8,128)} %get-tuple-element.9) | copy-start | bytes 248836

commit v3 on v2

--- a/solution.py
+++ b/solution.py
@@ -30,10 +30,10 @@
 
 def kernel(
     ns, nc, scale,
-    field_hbm, grad_hbm, filt_hbm, gf_ref, gw_ref,
-    field_ref, grad_ref, filt_ref,
+    field_hbm, grad_hbm, filt_hbm, gf_hbm, gw_hbm,
+    field_ref, grad_ref, filt_ref, gf_ref, gw_ref,
     wide, wire, halo_own, halo_in, g, fa, wm, field_acc, parts, rs, total,
-    in_sem, z_send, z_recv, h_send, h_recv, rs_send, rs_recv, ag_send, ag_recv,
+    in_sem, out_sem, z_send, z_recv, h_send, h_recv, rs_send, rs_recv, ag_send, ag_recv,
 ):
     s = lax.axis_index("space")
     c = lax.axis_index("chan")
@@ -46,8 +46,8 @@
     ]
     for load in loads:
         load.start()
-    wire_rows = rows * cols // LANES
-    half = wire_rows // 2
+    span = rows // 2
+    half = span * cols // LANES
     nq = nc * PAD
     has_left, has_right = s > 0, s < ns - 1
     has_below, has_above = c > 0, c < nc - 1
@@ -84,96 +84,96 @@
     loads[0].wait()
     wide[:, :, :cols] = grad_ref[...].astype(F32)
     x = wide[...]
-    lane = lane_index((chans, 8, LANES))
-    tail = x[:, wire_rows:, :]
-    packed = jnp.concatenate(
-        [
-            jnp.where(lane < cols, x[:, 8 * t : 8 * t + 8, :], roll(tail, cols - 32 * t))
-            for t in range(wire_rows // 8)
-        ],
-        axis=1,
+    y = jnp.swapaxes(x, 0, 1)
+    lane = lane_index((chans, LANES))
+    left_over = span - half
+    for h in range(2):
+        packed = [
+            jnp.where(
+                lane < cols,
+                y[span * h + i],
+                roll(y[span * h + half + i % left_over], cols - 32 * (i // left_over)),
+            )
+            for i in range(half)
+        ]
+        wire[c, h] = jnp.stack(packed).reshape(half * chans, LANES).astype(BF16)
+
+    greeted = (ns - 1) + (nc - 1) * (
+        has_left.astype(jnp.int32) + has_right.astype(jnp.int32)
+    ) + has_below.astype(jnp.int32) + has_above.astype(jnp.int32)
+    pl.semaphore_wait(barrier, greeted)
+
+    def z_copy(up, t, h):
+        block = c - t if up else c + t
+        way = 0 if up else 1
+        return pltpu.make_async_remote_copy(
+            src_ref=wire.at[block, h],
+            dst_ref=wire.at[block, h],
+            send_sem=z_send.at[way, t, h],
+            recv_sem=z_recv.at[way, t, h],
+            device_id={"space": s, "chan": c + 1 if up else c - 1},
+            device_id_type=MESH,
+        )
+
+    def z_arrival(up, t, h):
+        block = c - 1 - t if up else c + 1 + t
+        way = 0 if up else 1
+        return pltpu.make_async_remote_copy(
+            src_ref=wire.at[block, h],
+            dst_ref=wire.at[block, h],
+            send_sem=z_send.at[way, t, h],
+            recv_sem=z_recv.at[way, t, h],
+            device_id={"space": s, "chan": c - 1 if up else c + 1},
+            device_id_type=MESH,
+        )
+
+    def sends(up, t):
+        if up:
+            return has_above & (c - t >= 0)
+        return has_below & (c + t < nc)
+
+    def arrives(up, t):
+        if up:
+            return c - 1 - t >= 0
+        return c + 1 + t < nc
+
+    def halo_copy(right, chan):
+        side = 0 if right else 1
+        return pltpu.make_async_remote_copy(
+            src_ref=halo_own,
+            dst_ref=halo_in.at[side, c],
+            send_sem=h_send.at[side, chan],
+            recv_sem=h_recv.at[side, c],
+            device_id={"space": s + 1 if right else s - 1, "chan": chan},
+            device_id_type=MESH,
+        )
+
+    def halo_arrival(side, block):
+        return pltpu.make_async_remote_copy(
+            src_ref=halo_own,
+            dst_ref=halo_in.at[side, block],
+            send_sem=h_send.at[side, block],
+            recv_sem=h_recv.at[side, block],
+            device_id={"space": s - 1 if side == 0 else s + 1, "chan": block},
+            device_id_type=MESH,
+        )
+
+    for h in range(2):
+        for up in (True, False):
+
+            @pl.when(sends(up, 0))
+            def _():
+                z_copy(up, 0, h).start()
+
+    place = lane_index(y.shape)
+    y = jnp.where(place < 2, y, 0.0) + roll(
+        jnp.where((place >= cols - 2) & (place < cols), y, 0.0), 30 - (cols - 2)
     )
-    packed = jnp.swapaxes(packed, 0, 1)
-    for h in range(2):
-        wire[c, h] = packed[h * half : (h + 1) * half].reshape(half * chans, LANES).astype(BF16)
-
-    lane = lane_index(x.shape)
-    y = jnp.where(lane < 2, x, 0.0) + roll(
-        jnp.where((lane >= cols - 2) & (lane < cols), x, 0.0), 30 - (cols - 2)
-    )
-    y = jnp.swapaxes(y, 0, 1)
     count = rows
     while count > 1:
         count //= 2
         y = y[:count] + roll(y[count:], 4 * count)
     halo_own[...] = row_pad(y)[0].astype(BF16)
-
-    greeted = (ns - 1) + (nc - 1) * (
-        has_left.astype(jnp.int32) + has_right.astype(jnp.int32)
-    ) + has_below.astype(jnp.int32) + has_above.astype(jnp.int32)
-    pl.semaphore_wait(barrier, greeted)
-
-    def z_copy(up, t, h):
-        block = c - t if up else c + t
-        way = 0 if up else 1
-        return pltpu.make_async_remote_copy(
-            src_ref=wire.at[block, h],
-            dst_ref=wire.at[block, h],
-            send_sem=z_send.at[way, t, h],
-            recv_sem=z_recv.at[way, t, h],
-            device_id={"space": s, "chan": c + 1 if up else c - 1},
-            device_id_type=MESH,
-        )
-
-    def z_arrival(up, t, h):
-        block = c - 1 - t if up else c + 1 + t
-        way = 0 if up else 1
-        return pltpu.make_async_remote_copy(
-            src_ref=wire.at[block, h],
-            dst_ref=wire.at[block, h],
-            send_sem=z_send.at[way, t, h],
-            recv_sem=z_recv.at[way, t, h],
-            device_id={"space": s, "chan": c - 1 if up else c + 1},
-            device_id_type=MESH,
-        )
-
-    def sends(up, t):
-        if up:
-            return has_above & (c - t >= 0)
-        return has_below & (c + t < nc)
-
-    def arrives(up, t):
-        if up:
-            return c - 1 - t >= 0
-        return c + 1 + t < nc
-
-    def halo_copy(right, chan):
-        side = 0 if right else 1
-        return pltpu.make_async_remote_copy(
-            src_ref=halo_own,
-            dst_ref=halo_in.at[side, c],
-            send_sem=h_send.at[side, chan],
-            recv_sem=h_recv.at[side, c],
-            device_id={"space": s + 1 if right else s - 1, "chan": chan},
-            device_id_type=MESH,
-        )
-
-    def halo_arrival(side, block):
-        return pltpu.make_async_remote_copy(
-            src_ref=halo_own,
-            dst_ref=halo_in.at[side, block],
-            send_sem=h_send.at[side, block],
-            recv_sem=h_recv.at[side, block],
-            device_id={"space": s - 1 if side == 0 else s + 1, "chan": block},
-            device_id_type=MESH,
-        )
-
-    for h in range(2):
-        for up in (True, False):
-
-            @pl.when(sends(up, 0))
-            def _():
-                z_copy(up, 0, h).start()
 
     for right, there in ((True, has_right), (False, has_left)):
 
@@ -224,33 +224,35 @@
         g[block, 0:2] = jnp.zeros((2, PAD, LANES), BF16)
         g[block, rows + 2 :] = jnp.zeros((2, PAD, LANES), BF16)
 
-    def unpack(block):
-        for side, there in ((0, has_left), (1, has_right)):
-
-            @pl.when(there)
-            def _():
-                halo_arrival(side, block).wait_recv()
-
-        w = jnp.concatenate(
-            [wire[block, h].astype(F32).reshape(half, chans, LANES) for h in range(2)], axis=0
-        )
-        lane = lane_index((chans, LANES))
+    def unpack(block, h):
+        if h == 0:
+            for side, there in ((0, has_left), (1, has_right)):
+
+                @pl.when(there)
+                def _():
+                    halo_arrival(side, block).wait_recv()
+
+        w = wire[block, h].astype(F32).reshape(half, chans, LANES)
         left = halo_in[0, block].astype(F32)[:chans]
         right = halo_in[1, block].astype(F32)[:chans]
         border = jnp.where(lane % 4 < 2, right, left)
         edge = ((lane >= cols) & (lane < cols + 2)) | (lane >= LANES - 2)
-        out = []
-        for r in range(rows):
-            if r < wire_rows:
-                main = w[r]
+        placed = []
+        for i in range(span):
+            if i < half:
+                main = w[i]
             else:
-                j = r - wire_rows
-                main = jnp.zeros((chans, LANES), F32)
-                for t in range(cols // 32):
-                    main = jnp.where(lane // 32 == t, roll(w[8 * t + j], 32 * t - cols), main)
-            rim = jnp.where(edge, roll(border, cols - 4 * r), 0.0)
-            out.append(jnp.where(lane < cols, main, rim))
-        g[block, 2 : 2 + rows] = row_pad(jnp.stack(out)).astype(BF16)
+                main = roll(w[i - half], -cols)
+                for t in range(1, cols // 32):
+                    main = jnp.where(
+                        lane // 32 == t, roll(w[left_over * t + i - half], 32 * t - cols), main
+                    )
+            rim = jnp.where(edge, roll(border, cols - 4 * (span * h + i)), 0.0)
+            placed.append(jnp.where(lane < cols, main, rim))
+        g[block, 2 + span * h : 2 + span * (h + 1)] = row_pad(jnp.stack(placed)).astype(BF16)
+
+    def ready(h):
+        return range(0, span - 2, 2) if h == 0 else range(span - 2, rows, 2)
 
     def g_pair(block, r):
         return jnp.concatenate(
@@ -264,9 +266,9 @@
     n_tiles = 3 * chans // 8
     each = rs.shape[1]
 
-    def weight_gradient(block):
+    def weight_gradient(block, h):
         acc = jnp.zeros((3 * PAD, 3 * PAD), F32)
-        for r in range(0, rows, 2):
+        for r in ready(h):
             f_pair = jnp.concatenate(
                 [jnp.concatenate([fa[a, r], fa[a, r + 1]], axis=1) for a in range(3)], axis=0
             )
@@ -275,11 +277,12 @@
             )
         acc = acc.reshape(3, PAD, 3 * PAD)[:, :chans].reshape(n_tiles, 8, 3 * PAD)
         acc = jnp.concatenate([acc, jnp.zeros((n_tiles, 8, LANES - 3 * PAD), F32)], axis=2)
-        parts[pl.ds(block * n_tiles, n_tiles)] = acc
-
-    def field_gradient(block, first=False):
+        at = pl.ds(block * n_tiles, n_tiles)
+        parts[at] = acc if h == 0 else parts[at] + acc
+
+    def field_gradient(block, h, first=False):
         w = wm[block]
-        for r in range(0, rows, 2):
+        for r in ready(h):
             p = jnp.dot(w, g_pair(block, r), preferred_element_type=F32)
             field_acc[r // 2] = p if first else field_acc[r // 2] + p
 
@@ -320,10 +323,23 @@
             device_id_type=MESH,
         )
 
-    unpack(c)
-    weight_gradient(c)
-    field_gradient(c, first=True)
+    def work(block, h):
+        unpack(block, h)
+        weight_gradient(block, h)
+        field_gradient(block, h)
+
+    def both(t):
+        return arrives(True, t) & arrives(False, t)
+
+    def first_block(t):
+        above = c + 1 + t
+        return above - arrives(True, t).astype(jnp.int32) * (2 * t + 2)
+
     for t in range(nc - 1):
+        any_here = arrives(True, t) | arrives(False, t)
+        passes_on = sends(True, t + 1) | sends(False, t + 1)
+        late = t > 0 and 2 * (t - 1) <= nc - 3
+        last = t == nc - 2
         for h in range(2):
             for up in (True, False):
 
@@ -331,29 +347,46 @@
                 def _():
                     z_arrival(up, t, h).wait_recv()
 
-                if t + 1 < nc - 1:
+                if not last:
 
                     @pl.when(sends(up, t + 1))
                     def _():
                         z_copy(up, t + 1, h).start()
 
-        for up in (True, False):
-
-            @pl.when(arrives(up, t))
+            if t == 0:
+                unpack(c, h)
+                weight_gradient(c, h)
+                field_gradient(c, h, first=True)
+            if late:
+
+                @pl.when(both(t - 1))
+                def _():
+                    work(c + t, h)
+
+            if t > 0 and h == 0:
+
+                @pl.when(any_here if last else any_here & jnp.logical_not(passes_on))
+                def _():
+                    work(first_block(t), 0)
+
+        if t == 0 or not last:
+
+            @pl.when(any_here if t == 0 else any_here & passes_on)
             def _():
-                block = c - 1 - t if up else c + 1 + t
-                unpack(block)
-                weight_gradient(block)
-
-        if t + 1 == nc - 1:
+                work(first_block(t), 0)
+
+        @pl.when(any_here)
+        def _():
+            unpack(first_block(t), 1)
+            weight_gradient(first_block(t), 1)
+
+        if last:
             for d in range(1, ns):
                 rs_copy(d).start()
 
-        for up in (True, False):
-
-            @pl.when(arrives(up, t))
-            def _():
-                field_gradient(c - 1 - t if up else c + 1 + t)
+        @pl.when(any_here)
+        def _():
+            field_gradient(first_block(t), 1)
 
     def field_rows(first):
         out = []
@@ -372,8 +405,13 @@
         gf_ref[:, first : first + 8, :] = out[:, :, :cols]
 
     middle = rows // 2
+    def gf_out(i):
+        at = pl.ds(i * middle, middle)
+        return pltpu.make_async_copy(gf_ref.at[:, at], gf_hbm.at[:, at], out_sem.at[i])
+
     for first in range(0, middle, 8):
         field_rows(first)
+    gf_out(0).start()
 
     mine_total = parts[pl.ds(s * each, each)]
     for d in range(1, ns):
@@ -385,6 +423,7 @@
 
     for first in range(middle, rows, 8):
         field_rows(first)
+    gf_out(1).start()
 
     for d in range(1, ns):
         ag_arrival(d).wait_recv()
@@ -398,6 +437,9 @@
                 [block[a, :, b * PAD : b * PAD + chans] for block in blocks], axis=1
             )
 
+    gw_out = pltpu.make_async_copy(gw_ref, gw_hbm, out_sem.at[2])
+    gw_out.start()
+
     for t in range(nc - 1):
         for up in (True, False):
 
@@ -416,16 +458,29 @@
     for d in range(1, ns):
         rs_copy(d).wait_send()
         ag_copy(d).wait_send()
+    gf_out(0).wait()
+    gf_out(1).wait()
+    gw_out.wait()
+
+
+def keep(gf_in, gw_in, gf_out, gw_out, sem):
+    copies = [
+        pltpu.make_async_copy(gf_in, gf_out, sem.at[0]),
+        pltpu.make_async_copy(gw_in, gw_out, sem.at[1]),
+    ]
+    for copy in copies:
+        copy.start()
+    for copy in copies:
+        copy.wait()
 
 
 def per_device(ns, nc, field, grad_out, filters):
     chans, cols, rows = field.shape
-    wire_rows = rows * cols // LANES
     ch = filters.shape[1]
     n_tiles = nc * 3 * chans // 8
     each = -(-n_tiles // ns)
     scale = 1.0 / math.sqrt(rows * cols * ns)
-    vmem = pl.BlockSpec(memory_space=pltpu.VMEM)
+    hbm = pl.BlockSpec(memory_space=pltpu.HBM)
     dma = pltpu.SemaphoreType.DMA
     gf, gw = pl.pallas_call(
         functools.partial(kernel, ns, nc, scale),
@@ -433,14 +488,16 @@
             jax.ShapeDtypeStruct((chans, rows, cols), F32),
             jax.ShapeDtypeStruct((9, chans, ch), F32),
         ),
-        in_specs=[pl.BlockSpec(memory_space=pltpu.HBM)] * 3,
-        out_specs=(vmem, vmem),
+        in_specs=[hbm] * 3,
+        out_specs=(hbm, hbm),
         scratch_shapes=[
             pltpu.VMEM((chans, rows, cols), BF16),
             pltpu.VMEM((chans, rows, cols), BF16),
             pltpu.VMEM(filters.shape, BF16),
+            pltpu.VMEM((chans, rows, cols), F32),
+            pltpu.VMEM((9, chans, ch), F32),
             pltpu.VMEM((chans, rows, LANES), F32),
-            pltpu.VMEM((nc, 2, wire_rows // 2 * chans, LANES), BF16),
+            pltpu.VMEM((nc, 2, rows // 2 * cols // LANES * chans, LANES), BF16),
             pltpu.VMEM((PAD, LANES), BF16),
             pltpu.VMEM((2, nc, PAD, LANES), BF16),
             pltpu.VMEM((nc, rows + 4, PAD, LANES), BF16),
@@ -450,6 +507,7 @@
             pltpu.VMEM((ns * each, 8, LANES), F32),
             pltpu.VMEM((ns - 1, each, 8, LANES), F32),
             pltpu.VMEM((ns, each, 8, LANES), F32),
+            dma((3,)),
             dma((3,)),
             dma((2, nc - 1, 2)),
             dma((2, nc - 1, 2)),
@@ -467,6 +525,17 @@
             flops=4 * 9 * chans * ch * rows * cols, bytes_accessed=2 * 1024 * 1024, transcendentals=0
         ),
     )(jnp.swapaxes(field, 1, 2), jnp.swapaxes(grad_out, 1, 2), filters)
+    gf, gw = pl.pallas_call(
+        keep,
+        out_shape=(
+            jax.ShapeDtypeStruct(gf.shape, F32),
+            jax.ShapeDtypeStruct(gw.shape, F32),
+        ),
+        in_specs=[hbm] * 2,
+        out_specs=(hbm, hbm),
+        scratch_shapes=[dma((2,))],
+        compiler_params=pltpu.CompilerParams(vmem_limit_bytes=64 * 1024 * 1024),
+    )(gf, gw)
     return jnp.swapaxes(gf, 1, 2), gw
 
 

time: 31.6 us -> 45.5 us (1.44)
  Pallas kernels: 28.3 us -> 44.7 us
  local copies, waits for them, and re-layouts: 2.45 us -> 0 us
    pallas_call x0 -> x1, Pallas kernels: none -> 16.4 us  [per_device(): pl.pallas_call(keep, out_shape=(jax.ShapeDtypeStruct(gf.shape, F32), jax....]
    unnamed x4 -> x0, local copies, waits for them, and re-layouts: 2.45 us -> none
where the time goes in v3:
time: 45.5 us; the launch traced here: 45.3 us
  Pallas kernels  44.7 us (98%)
  between operations  0.64 us (1%)
    pallas_call x1, Pallas kernels, per_device(): pl.pallas_call(functools.partial(kernel, ns, nc, scale), out_shape=(jax.S...  28.3 us
    pallas_call x1, Pallas kernels, per_device(): pl.pallas_call(keep, out_shape=(jax.ShapeDtypeStruct(gf.shape, F32), jax....  16.4 us

profile of v3, /device:TPU:0, one launch (start us, length us, event | category | flops | bytes accessed | tf_op | source)
XLA Modules:
  0.0 45.3 jit_solution(18094733692015297941)
XLA Ops:
  0.6 28.3 %shard_map.50 = (f32[24,32,96]{2,1,0:T(8,128)}, f32[9,24,96]{2,1,0:T(8,128)}) custom-call(bf16[24,32,96]{2,1,0:T(8,128)(2,1)} %bitcast.4, bf16[24,32,96]{2,1,0:T(8,128)(2,1)} %bitcast.5, bf16[9,96,96]{2,1,0:T(8,128)(2,1)} %filt_hbm.1), custom_call_target="tpu_custom_call" | custom-call | flops 254803968 | bytes 2097152 | tf_op jit(solution)/shard_map/pallas_call | solution.py:485
  29.0 16.4 %shard_map.51 = (f32[24,32,96]{2,1,0:T(8,128)}, f32[9,24,96]{2,1,0:T(8,128)}) custom-call(f32[24,32,96]{2,1,0:T(8,128)} %get-tuple-element.6.gf_in, f32[9,24,96]{2,1,0:T(8,128)} %get-tuple-element.7.gw_in), custom_call_target="tpu_custom_call" | custom-call | tf_op jit(solution)/shard_map/pallas_call | solution.py:528

commit v4 on v3

--- a/solution.py
+++ b/solution.py
@@ -252,39 +252,39 @@
         g[block, 2 + span * h : 2 + span * (h + 1)] = row_pad(jnp.stack(placed)).astype(BF16)
 
     def ready(h):
-        return range(0, span - 2, 2) if h == 0 else range(span - 2, rows, 2)
-
-    def g_pair(block, r):
+        return range(0, span - 2) if h == 0 else range(span - 2, rows)
+
+    def g_rows(block, h):
         return jnp.concatenate(
             [
-                jnp.concatenate([g[block, r + 4 - 2 * b], g[block, r + 5 - 2 * b]], axis=1)
+                jnp.concatenate([g[block, r + 4 - 2 * b] for r in ready(h)], axis=1)
                 for b in range(3)
             ],
             axis=0,
         )
 
+    def f_rows(h):
+        return jnp.concatenate(
+            [jnp.concatenate([fa[a, r] for r in ready(h)], axis=1) for a in range(3)], axis=0
+        )
+
     n_tiles = 3 * chans // 8
     each = rs.shape[1]
 
     def weight_gradient(block, h):
-        acc = jnp.zeros((3 * PAD, 3 * PAD), F32)
-        for r in ready(h):
-            f_pair = jnp.concatenate(
-                [jnp.concatenate([fa[a, r], fa[a, r + 1]], axis=1) for a in range(3)], axis=0
-            )
-            acc = acc + lax.dot_general(
-                f_pair, g_pair(block, r), (((1,), (1,)), ((), ())), preferred_element_type=F32
-            )
+        acc = lax.dot_general(
+            f_rows(h), g_rows(block, h), (((1,), (1,)), ((), ())), preferred_element_type=F32
+        )
         acc = acc.reshape(3, PAD, 3 * PAD)[:, :chans].reshape(n_tiles, 8, 3 * PAD)
         acc = jnp.concatenate([acc, jnp.zeros((n_tiles, 8, LANES - 3 * PAD), F32)], axis=2)
         at = pl.ds(block * n_tiles, n_tiles)
         parts[at] = acc if h == 0 else parts[at] + acc
 
     def field_gradient(block, h, first=False):
-        w = wm[block]
-        for r in ready(h):
-            p = jnp.dot(w, g_pair(block, r), preferred_element_type=F32)
-            field_acc[r // 2] = p if first else field_acc[r // 2] + p
+        p = jnp.dot(wm[block], g_rows(block, h), preferred_element_type=F32)
+        for i, r in enumerate(ready(h)):
+            here = p[:, i * LANES : (i + 1) * LANES]
+            field_acc[r] = here if first else field_acc[r] + here
 
     spare = ns * each - nc * n_tiles
     if spare:
@@ -390,17 +390,11 @@
 
     def field_rows(first):
         out = []
-        for r in range(first, first + 8, 2):
-            p = field_acc[r // 2]
-            for j in range(2):
-                part = p[:, j * LANES : (j + 1) * LANES]
-                out.append(
-                    sum(
-                        roll(part[a * chans : (a + 1) * chans], 2 * (a - 1)) if a != 1
-                        else part[a * chans : (a + 1) * chans]
-                        for a in range(3)
-                    )
-                )
+        for r in range(first, first + 8):
+            p = field_acc[r]
+            out.append(
+                roll(p[:chans], -2) + p[chans : 2 * chans] + roll(p[2 * chans :], 2)
+            )
         out = jnp.swapaxes(jnp.stack(out), 0, 1)
         gf_ref[:, first : first + 8, :] = out[:, :, :cols]
 
@@ -463,14 +457,22 @@
     gw_out.wait()
 
 
-def keep(gf_in, gw_in, gf_out, gw_out, sem):
-    copies = [
-        pltpu.make_async_copy(gf_in, gf_out, sem.at[0]),
-        pltpu.make_async_copy(gw_in, gw_out, sem.at[1]),
-    ]
-    for copy in copies:
+def keep(gf_in, gw_in, gf_out, gw_out, gf, gw, in_sem, out_sem):
+    pieces = in_sem.shape[0] - 1
+    step = gf.shape[0] // pieces
+    ins, outs = [], []
+    for i in range(pieces):
+        at = pl.ds(i * step, step)
+        ins.append(pltpu.make_async_copy(gf_in.at[at], gf.at[at], in_sem.at[i]))
+        outs.append(pltpu.make_async_copy(gf.at[at], gf_out.at[at], out_sem.at[i]))
+    ins.append(pltpu.make_async_copy(gw_in, gw, in_sem.at[pieces]))
+    outs.append(pltpu.make_async_copy(gw, gw_out, out_sem.at[pieces]))
+    for copy in ins:
         copy.start()
-    for copy in copies:
+    for there, back in zip(ins, outs):
+        there.wait()
+        back.start()
+    for copy in outs:
         copy.wait()
 
 
@@ -503,7 +505,7 @@
             pltpu.VMEM((nc, rows + 4, PAD, LANES), BF16),
             pltpu.VMEM((3, rows, PAD, LANES), BF16),
             pltpu.VMEM((nc, 3 * chans, 3 * PAD), BF16),
-            pltpu.VMEM((rows // 2, 3 * chans, 2 * LANES), F32),
+            pltpu.VMEM((rows, 3 * chans, LANES), F32),
             pltpu.VMEM((ns * each, 8, LANES), F32),
             pltpu.VMEM((ns - 1, each, 8, LANES), F32),
             pltpu.VMEM((ns, each, 8, LANES), F32),
@@ -533,7 +535,9 @@
         ),
         in_specs=[hbm] * 2,
         out_specs=(hbm, hbm),
-        scratch_shapes=[dma((2,))],
+        scratch_shapes=[
+            pltpu.VMEM(gf.shape, F32), pltpu.VMEM(gw.shape, F32), dma((4,)), dma((4,)),
+        ],
         compiler_params=pltpu.CompilerParams(vmem_limit_bytes=64 * 1024 * 1024),
     )(gf, gw)
     return jnp.swapaxes(gf, 1, 2), gw

time: 45.5 us -> 30.9 us (0.68)
  Pallas kernels: 44.7 us -> 30.1 us
    pallas_call x1, Pallas kernels: 16.4 us -> 1.8 us  [per_device(): pl.pallas_call(keep, out_shape=(jax.ShapeDtypeStruct(gf.shape, F32), jax....]
where the time goes in v4:
time: 30.9 us; the launch traced here: 30.8 us
  Pallas kernels  30.1 us (97%)
  between operations  0.64 us (2%)
    pallas_call x1, Pallas kernels, per_device(): pl.pallas_call(functools.partial(kernel, ns, nc, scale), out_shape=(jax.S...  28.3 us
    pallas_call x1, Pallas kernels, per_device(): pl.pallas_call(keep, out_shape=(jax.ShapeDtypeStruct(gf.shape, F32), jax....  1.8 us

profile of v4, /device:TPU:0, one launch (start us, length us, event | category | flops | bytes accessed | tf_op | source)
XLA Modules:
  0.0 30.8 jit_solution(8404629399778383494)
XLA Ops:
  0.6 28.3 %shard_map.50 = (f32[24,32,96]{2,1,0:T(8,128)}, f32[9,24,96]{2,1,0:T(8,128)}) custom-call(bf16[24,32,96]{2,1,0:T(8,128)(2,1)} %bitcast.4, bf16[24,32,96]{2,1,0:T(8,128)(2,1)} %bitcast.5, bf16[9,96,96]{2,1,0:T(8,128)(2,1)} %filt_hbm.1), custom_call_target="tpu_custom_call" | custom-call | flops 254803968 | bytes 2097152 | tf_op jit(solution)/shard_map/pallas_call | solution.py:487
  29.0 1.8 %shard_map.51 = (f32[24,32,96]{2,1,0:T(8,128)}, f32[9,24,96]{2,1,0:T(8,128)}) custom-call(f32[24,32,96]{2,1,0:T(8,128)} %get-tuple-element.6.gf_in, f32[9,24,96]{2,1,0:T(8,128)} %get-tuple-element.7.gw_in), custom_call_target="tpu_custom_call" | custom-call | tf_op jit(solution)/shard_map/pallas_call | solution.py:530

commit v5 on v4

--- a/solution.py
+++ b/solution.py
@@ -140,7 +140,7 @@
     def halo_copy(right, chan):
         side = 0 if right else 1
         return pltpu.make_async_remote_copy(
-            src_ref=halo_own,
+            src_ref=halo_own.at[side],
             dst_ref=halo_in.at[side, c],
             send_sem=h_send.at[side, chan],
             recv_sem=h_recv.at[side, c],
@@ -150,7 +150,7 @@
 
     def halo_arrival(side, block):
         return pltpu.make_async_remote_copy(
-            src_ref=halo_own,
+            src_ref=halo_own.at[side],
             dst_ref=halo_in.at[side, block],
             send_sem=h_send.at[side, block],
             recv_sem=h_recv.at[side, block],
@@ -173,7 +173,13 @@
     while count > 1:
         count //= 2
         y = y[:count] + roll(y[count:], 4 * count)
-    halo_own[...] = row_pad(y)[0].astype(BF16)
+    ends = y[0]
+    fold = halo_own.shape[1]
+    filler = jnp.zeros((2 * fold - chans, LANES), F32)
+    for side in range(2):
+        kept = jnp.where((lane % 4 < 2) == (side == 1), ends, 0.0)
+        rest = jnp.concatenate([roll(kept[fold:], 2 if side else -2), filler], axis=0)
+        halo_own[side] = (kept[:fold] + rest).astype(BF16)
 
     for right, there in ((True, has_right), (False, has_left)):
 
@@ -233,8 +239,10 @@
                     halo_arrival(side, block).wait_recv()
 
         w = wire[block, h].astype(F32).reshape(half, chans, LANES)
-        left = halo_in[0, block].astype(F32)[:chans]
-        right = halo_in[1, block].astype(F32)[:chans]
+        left, right = halo_in[0, block].astype(F32), halo_in[1, block].astype(F32)
+        more = chans - left.shape[0]
+        left = jnp.concatenate([left, roll(left[:more], 2)], axis=0)
+        right = jnp.concatenate([right, roll(right[:more], -2)], axis=0)
         border = jnp.where(lane % 4 < 2, right, left)
         edge = ((lane >= cols) & (lane < cols + 2)) | (lane >= LANES - 2)
         placed = []
@@ -500,8 +508,8 @@
             pltpu.VMEM((9, chans, ch), F32),
             pltpu.VMEM((chans, rows, LANES), F32),
             pltpu.VMEM((nc, 2, rows // 2 * cols // LANES * chans, LANES), BF16),
-            pltpu.VMEM((PAD, LANES), BF16),
-            pltpu.VMEM((2, nc, PAD, LANES), BF16),
+            pltpu.VMEM((2, PAD // 2, LANES), BF16),
+            pltpu.VMEM((2, nc, PAD // 2, LANES), BF16),
             pltpu.VMEM((nc, rows + 4, PAD, LANES), BF16),
             pltpu.VMEM((3, rows, PAD, LANES), BF16),
             pltpu.VMEM((nc, 3 * chans, 3 * PAD), BF16),

time: 30.9 us -> 30.5 us (0.987)
  Pallas kernels: 30.1 us -> 29.7 us
    pallas_call x1, Pallas kernels: 28.3 us -> 27.9 us  [per_device(): pl.pallas_call(functools.partial(kernel, ns, nc, scale), out_shape=(jax.S...]
where the time goes in v5:
time: 30.5 us; the launch traced here: 30.3 us
  Pallas kernels  29.7 us (97%)
  between operations  0.64 us (2%)
    pallas_call x1, Pallas kernels, per_device(): pl.pallas_call(functools.partial(kernel, ns, nc, scale), out_shape=(jax.S...  27.9 us
    pallas_call x1, Pallas kernels, per_device(): pl.pallas_call(keep, out_shape=(jax.ShapeDtypeStruct(gf.shape, F32), jax....  1.8 us

profile of v5, /device:TPU:0, one launch (start us, length us, event | category | flops | bytes accessed | tf_op | source)
XLA Modules:
  0.0 30.3 jit_solution(15933463135291035085)
XLA Ops:
  0.6 27.9 %shard_map.50 = (f32[24,32,96]{2,1,0:T(8,128)}, f32[9,24,96]{2,1,0:T(8,128)}) custom-call(bf16[24,32,96]{2,1,0:T(8,128)(2,1)} %bitcast.4, bf16[24,32,96]{2,1,0:T(8,128)(2,1)} %bitcast.5, bf16[9,96,96]{2,1,0:T(8,128)(2,1)} %filt_hbm.1), custom_call_target="tpu_custom_call" | custom-call | flops 254803968 | bytes 2097152 | tf_op jit(solution)/shard_map/pallas_call | solution.py:495
  28.5 1.8 %shard_map.51 = (f32[24,32,96]{2,1,0:T(8,128)}, f32[9,24,96]{2,1,0:T(8,128)}) custom-call(f32[24,32,96]{2,1,0:T(8,128)} %get-tuple-element.6.gf_in, f32[9,24,96]{2,1,0:T(8,128)} %get-tuple-element.7.gw_in), custom_call_target="tpu_custom_call" | custom-call | tf_op jit(solution)/shard_map/pallas_call | solution.py:538
